TPU v7x, 512 devices: a whole 4x8x8 slice. The times are simulated.
512 devices in a mesh: grp: 4 (over x), gx: 16 (over y, core), gy: 8 (over z).
Axes of the slice: x: 4, y: 8, z: 8, core: 2. Of those that a mesh axis runs over, the one named last changes fastest.
Arguments:
- source: float32 [256, 128, 512], P('gx', 'gy', 'grp'), may hold values from -13 to 13
- conductance: float32 [256, 128, 512], P('gx', 'gy', 'grp'), may hold values from 0.2 to 5
- storage: float32 [256, 128, 512], P('gx', 'gy', 'grp'), may hold values from 0.05 to 1
- aggregate_ids: int32 [256, 128, 512], P('gx', 'gy', 'grp'), may hold values from 0 to 511, as said below
- coarse_values: float32 [4096, 64, 256], P(('grp', 'gx', 'gy')), as said below
- coarse_columns: int32 [4096, 4], P(('grp', 'gx', 'gy')), may hold values from 0 to 4095, as said below
Outputs:
- solution: float32 [256, 128, 512], P('gx', 'gy', 'grp')
- coarse_error: float32 [262144], P(('grp', 'gx', 'gy'))
Inputs may be any that keep to these rules, and one draw needn't show every extreme that they name: `aggregate_ids`: on each device, every id names exactly the 64 cells of one aligned 4 x 4 x 4 box of the device's block, and different boxes have different ids. `coarse_columns`: entry 0 of block row b is b itself; every other entry names a block of a device whose gx and gy indices differ from those of row b's device by at most one. `coarse_values`: in every row of the coarse operator the diagonal entry of the first stored block exceeds the sum of the magnitudes of all other stored entries of that row.
All inputs are finite; a program needn't handle non-finite values.
Results may differ from a plain program's by a relative error of at most 0.0001.
Values sent between devices are 32-bit elements; how exact they have to be, the bound alone decides.
A program may use at most 64 MiB of HBM per device.

v0:
```python
import jax
import jax.numpy as jnp
from jax import lax
from jax.sharding import PartitionSpec as P

NU = 2
CITER = 4
WEIGHT = 2.0 / 3.0
PAIRS = ((0, 1), (0, -1), (1, 1), (1, -1), (2, 1), (2, -1))


def padded_2(cells, sides, width):
    for axis, dim in sides:
        count = lax.axis_size(axis)
        ends = count - 1
        head = lax.slice_in_dim(cells, 0, width, axis=dim)
        tail = lax.slice_in_dim(cells, cells.shape[dim] - width, cells.shape[dim], axis=dim)
        cells = jnp.concatenate(
            [
                lax.ppermute(tail, axis, [(i, (i + 1) % count) for i in range(ends)]),
                cells,
                lax.ppermute(head, axis, [((i + 1) % count, i) for i in range(ends)]),
            ],
            axis=dim,
        )
    return cells


def shifted(padded, dimension, offset):
    window = [slice(1, -1), slice(1, -1), slice(1, -1)]
    window[dimension] = slice(1 + offset, padded.shape[dimension] - 1 + offset)
    return padded[tuple(window)]


def trimmed(array):
    return array[1:-1, 1:-1, 1:-1]


def apply_wide(padded_field, storage_part, face_part):
    center = trimmed(padded_field)
    summed = storage_part * center
    for position in range(6):
        dimension, offset = PAIRS[position]
        summed = summed + face_part[position] * (center - shifted(padded_field, dimension, offset))
    return summed


def face_terms(padded_cond):
    center = trimmed(padded_cond)
    return [0.5 * (center + shifted(padded_cond, dimension, offset)) for dimension, offset in PAIRS]


def add_faces(storage_part, face_part):
    running = storage_part
    for position in range(6):
        running = running + face_part[position]
    return running


def local(source, conductance, storage, aggregate_ids, coarse_values, coarse_columns):
    size_x, size_y, size_z = source.shape
    padded_cond = padded_2(conductance, (("grp", 2), ("gx", 0), ("gy", 1)), 1)
    face_list = face_terms(padded_cond)
    diagonal = add_faces(storage, face_list)

    def operate(field):
        padded = padded_2(field, (("grp", 2), ("gx", 0), ("gy", 1)), 1)
        return apply_wide(padded, storage, face_list)

    solution = WEIGHT * source / diagonal
    solution = solution + WEIGHT * (source - operate(solution)) / diagonal
    residual = source - operate(solution)
    smoothed = residual - WEIGHT * operate(residual / diagonal)
    box_labels = aggregate_ids[::4, ::4, ::4].reshape(-1)
    box_totals = (
        smoothed.reshape(size_x // 4, 4, size_y // 4, 4, size_z // 4, 4)
        .sum(axis=(1, 3, 5))
        .reshape(-1)
    )
    coarse_rhs = jnp.zeros(box_totals.shape, source.dtype).at[box_labels].set(box_totals)
    coarse_diag = jnp.diagonal(coarse_values[:, :, :64], axis1=1, axis2=2).reshape(-1)
    coarse_error = coarse_rhs / coarse_diag
    for sweep_number in range(CITER - 1):
        gathered = lax.all_gather(coarse_error, ("grp", "gx", "gy"), axis=0, tiled=True)
        blocks = gathered.reshape(-1, 64)[coarse_columns]
        blocks = blocks.reshape(blocks.shape[0], -1)
        applied = jnp.einsum(
            "bim,bm->bi", coarse_values, blocks, precision=lax.Precision.HIGHEST
        ).reshape(-1)
        coarse_error = coarse_error + (coarse_rhs - applied) / coarse_diag
    small_field = coarse_error[box_labels].reshape(size_x // 4, size_y // 4, size_z // 4)
    lifted = jnp.repeat(jnp.repeat(jnp.repeat(small_field, 4, axis=0), 4, axis=1), 4, axis=2)
    solution = solution + (lifted - WEIGHT * operate(lifted) / diagonal)
    for sweep_number in range(NU):
        solution = solution + WEIGHT * (source - operate(solution)) / diagonal
    return (solution, coarse_error)


def solution(mesh):
    return jax.shard_map(
        local,
        mesh=mesh,
        in_specs=(
            P("gx", "gy", "grp"),
            P("gx", "gy", "grp"),
            P("gx", "gy", "grp"),
            P("gx", "gy", "grp"),
            P(("grp", "gx", "gy"), None, None),
            P(("grp", "gx", "gy"), None),
        ),
        out_specs=(P("gx", "gy", "grp"), P(("grp", "gx", "gy"))),
        check_vma=False,
    )
```

profile of v0, /device:TPU:224, one launch (start us, length us, event | category | flops | bytes accessed | tf_op | source)
XLA Modules:
  0.0 583.4 jit_solution(13674778865393548589)
XLA Ops:
  8.3 3.5 collective-permute-start
  14.6 4.1 collective-permute-done.1
  19.5 1.9 collective-permute-start.2
  21.4 2.4 collective-permute-start.3
  23.9 3.8 collective-permute-done.3
  28.8 1.9 collective-permute-start.4
  30.7 5.5 collective-permute-start.5
  37.6 2.0 fusion.140
  39.8 3.4 collective-permute-start.6
  45.7 4.4 collective-permute-done.7
  50.1 1.9 collective-permute-start.8
  52.0 2.4 collective-permute-start.9
  54.5 3.8 collective-permute-done.9
  58.5 1.9 collective-permute-start.10
  60.4 5.4 collective-permute-start.11
  67.7 3.1 collective-permute-start.12
  73.4 4.4 collective-permute-done.13
  77.8 2.1 collective-permute-start.14
  79.9 2.4 collective-permute-start.15
  82.3 3.8 collective-permute-done.15
  86.3 1.9 collective-permute-start.16
  88.2 5.4 collective-permute-start.17
  95.6 1.9 collective-permute-start.18
  100.8 3.6 collective-permute-done.19
  104.4 1.9 collective-permute-start.20
  106.4 2.4 collective-permute-start.21
  108.8 3.8 collective-permute-done.21
  112.8 1.9 collective-permute-start.22
  114.7 5.4 collective-permute-start.23
  120.2 2.0 copy.270
  124.4 5.7 reshape.84
  130.1 2.6 reduce_sum.9
  132.8 2.4 scatter_custom_fusion
  136.1 108.1 %all-gather.7.cloned.1.call-done = f32[512,1,512]{2,1,0:T(1,128)} async-done(((f32[1,1,512]{2,1,0:T(1,128)}), f32[512,1,512]{2,1,0:T(1,128)}) %all-gather.7.cloned.1.call-update) | async-done | bytes 1048592 | tf_op jit(solution)/shard_map/all_gather | solution.py:84
  244.2 3.8 reduce
  249.8 2.2 gather_fusion.1
  253.5 109.6 %all-gather.9.cloned.1.call-done = f32[512,1,512]{2,1,0:T(1,128)} async-done(((f32[1,1,512]{2,1,0:T(1,128)}), f32[512,1,512]{2,1,0:T(1,128)}) %all-gather.9.cloned.1.call-update) | async-done | bytes 1048592 | tf_op jit(solution)/shard_map/all_gather | solution.py:84
  363.1 3.8 reduce.1
  368.7 2.2 gather_fusion.2
  372.1 109.8 %all-gather.11.cloned.1.call-done = f32[512,1,512]{2,1,0:T(1,128)} async-done(((f32[1,1,512]{2,1,0:T(1,128)}), f32[512,1,512]{2,1,0:T(1,128)}) %all-gather.11.cloned.1.call-update) | async-done | bytes 1048592 | tf_op jit(solution)/shard_map/all_gather | solution.py:84
  482.0 3.8 reduce.2
  487.5 2.2 gather_fusion.3
  490.4 3.5 gather_fusion.4
  494.3 3.3 collective-permute-start.24
  499.5 3.6 collective-permute-done.25
  503.4 1.9 collective-permute-start.26
  505.3 2.4 collective-permute-start.27
  507.7 3.8 collective-permute-done.27
  511.7 2.8 collective-permute-start.28
  514.5 4.3 collective-permute-start.29
  520.7 3.4 collective-permute-start.30
  526.6 4.4 collective-permute-done.31
  531.0 1.9 collective-permute-start.32
  533.0 2.4 collective-permute-start.33
  535.4 3.8 collective-permute-done.33
  539.4 2.3 collective-permute-start.34
  541.7 5.0 collective-permute-start.35
  548.7 3.1 collective-permute-start.36
  554.3 4.4 collective-permute-done.37
  558.7 1.9 collective-permute-start.38
  560.6 2.4 collective-permute-start.39
  563.1 3.8 collective-permute-done.39
  567.1 1.9 collective-permute-start.40
  569.0 5.4 collective-permute-start.41
  (124 shorter events, 46.3 us)
Async XLA Ops:
  7.2 237.0 %all-gather.7.cloned.1.call-start = ((), (), s32[]{:S(2)}) async-start(), calls=%async_computation | async-start | bytes 1050624 | tf_op jit(solution)/shard_map/all_gather | solution.py:84
  8.3 59.0 %copy-start.1 = (f32[16,16,128]{2,1,0:T(8,128)S(1)}, f32[16,16,128]{2,1,0:T(8,128)}, u32[]{:S(2)}) copy-start(f32[16,16,128]{2,1,0:T(8,128)} %param.8) | copy-start | bytes 393220
  8.3 59.0 %copy-start.3 = (f32[16,16,128]{2,1,0:T(8,128)S(1)}, f32[16,16,128]{2,1,0:T(8,128)}, u32[]{:S(2)}) copy-start(f32[16,16,128]{2,1,0:T(8,128)} %param.6) | copy-start | bytes 393220
  8.3 6.3 %collective-permute-start = (f32[16,16,1]{2,1,0:T(8,128)S(1)}, f32[16,16,1]{2,1,0:T(8,128)S(1)}, u32[]{:S(2)}, u32[]{:S(2)}) collective-permute-start(f32[16,16,1]{2,1,0:T(8,128)S(1)} %get-tuple-element.55), channel_id=1, source_target_pairs={{0,128},{128,256},{256,384},{1,129},{129,257},{257,385},{2,130},{1... | collective-permute-start | bytes 3080 | tf_op jit(solution)/shard_map/ppermute | solution.py:20
  11.9 6.9 %collective-permute-start.1 = (f32[16,16,1]{2,1,0:T(8,128)S(1)}, f32[16,16,1]{2,1,0:T(8,128)S(1)}, u32[]{:S(2)}, u32[]{:S(2)}) collective-permute-start(f32[16,16,1]{2,1,0:T(8,128)S(1)} %get-tuple-element.56), channel_id=1, source_target_pairs={{128,0},{256,128},{384,256},{129,1},{257,129},{385,257},{130,2},{2... | collective-permute-start | bytes 3080 | tf_op jit(solution)/shard_map/ppermute | solution.py:22
  19.5 4.3 collective-permute-start.2
  21.4 6.3 %collective-permute-start.3 = (f32[1,16,130]{2,1,0:T(8,128)S(1)}, f32[1,16,130]{2,1,0:T(8,128)S(1)}, u32[]{:S(2)}, u32[]{:S(2)}) collective-permute-start(f32[1,16,130]{2,1,0:T(8,128)S(1)} %get-tuple-element.43), channel_id=1, source_target_pairs={{0,8},{8,16},{16,24},{24,32},{32,40},{40,48},{48,56},{56,64},{64,7... | collective-permute-start | bytes 24968 | tf_op jit(solution)/shard_map/ppermute | solution.py:20
  28.8 7.4 %collective-permute-start.4 = (f32[18,1,130]{2,1,0:T(1,128)S(1)}, f32[18,1,130]{2,1,0:T(1,128)S(1)}, u32[]{:S(2)}, u32[]{:S(2)}) collective-permute-start(f32[18,1,130]{2,1,0:T(1,128)S(1)} %get-tuple-element.30), channel_id=1, source_target_pairs={{1,0},{2,1},{3,2},{4,3},{5,4},{6,5},{7,6},{9,8},{10,9},{11,10},{12... | collective-permute-start | bytes 28088 | tf_op jit(solution)/shard_map/ppermute | solution.py:22
  30.7 6.9 %collective-permute-start.5 = (f32[18,1,130]{2,1,0:T(1,128)S(1)}, f32[18,1,130]{2,1,0:T(1,128)S(1)}, u32[]{:S(2)}, u32[]{:S(2)}) collective-permute-start(f32[18,1,130]{2,1,0:T(1,128)S(1)} %get-tuple-element.29), channel_id=1, source_target_pairs={{0,1},{1,2},{2,3},{3,4},{4,5},{5,6},{6,7},{8,9},{9,10},{10,11},{11... | collective-permute-start | bytes 28088 | tf_op jit(solution)/shard_map/ppermute | solution.py:20
  39.8 5.9 %collective-permute-start.6 = (f32[16,16,1]{2,1,0:T(8,128)S(1)}, f32[16,16,1]{2,1,0:T(8,128)S(1)}, u32[]{:S(2)}, u32[]{:S(2)}) collective-permute-start(f32[16,16,1]{2,1,0:T(8,128)S(1)} %get-tuple-element.54), channel_id=1, source_target_pairs={{0,128},{128,256},{256,384},{1,129},{129,257},{257,385},{2,130},{1... | collective-permute-start | bytes 3080 | tf_op jit(solution)/shard_map/ppermute | solution.py:20
  43.2 6.9 %collective-permute-start.7 = (f32[16,16,1]{2,1,0:T(8,128)S(1)}, f32[16,16,1]{2,1,0:T(8,128)S(1)}, u32[]{:S(2)}, u32[]{:S(2)}) collective-permute-start(f32[16,16,1]{2,1,0:T(8,128)S(1)} %get-tuple-element.53), channel_id=1, source_target_pairs={{128,0},{256,128},{384,256},{129,1},{257,129},{385,257},{130,2},{2... | collective-permute-start | bytes 3080 | tf_op jit(solution)/shard_map/ppermute | solution.py:22
  50.1 4.3 collective-permute-start.8
  52.0 6.3 %collective-permute-start.9 = (f32[1,16,130]{2,1,0:T(8,128)S(1)}, f32[1,16,130]{2,1,0:T(8,128)S(1)}, u32[]{:S(2)}, u32[]{:S(2)}) collective-permute-start(f32[1,16,130]{2,1,0:T(8,128)S(1)} %get-tuple-element.41), channel_id=1, source_target_pairs={{0,8},{8,16},{16,24},{24,32},{32,40},{40,48},{48,56},{56,64},{64,7... | collective-permute-start | bytes 24968 | tf_op jit(solution)/shard_map/ppermute | solution.py:20
  58.5 7.4 %collective-permute-start.10 = (f32[18,1,130]{2,1,0:T(1,128)S(1)}, f32[18,1,130]{2,1,0:T(1,128)S(1)}, u32[]{:S(2)}, u32[]{:S(2)}) collective-permute-start(f32[18,1,130]{2,1,0:T(1,128)S(1)} %get-tuple-element.27), channel_id=1, source_target_pairs={{1,0},{2,1},{3,2},{4,3},{5,4},{6,5},{7,6},{9,8},{10,9},{11,10},{12... | collective-permute-start | bytes 28088 | tf_op jit(solution)/shard_map/ppermute | solution.py:22
  60.4 6.9 %collective-permute-start.11 = (f32[18,1,130]{2,1,0:T(1,128)S(1)}, f32[18,1,130]{2,1,0:T(1,128)S(1)}, u32[]{:S(2)}, u32[]{:S(2)}) collective-permute-start(f32[18,1,130]{2,1,0:T(1,128)S(1)} %get-tuple-element.28), channel_id=1, source_target_pairs={{0,1},{1,2},{2,3},{3,4},{4,5},{5,6},{6,7},{8,9},{9,10},{10,11},{11... | collective-permute-start | bytes 28088 | tf_op jit(solution)/shard_map/ppermute | solution.py:20
  67.7 5.6 collective-permute-start.12
  70.9 6.9 %collective-permute-start.13 = (f32[16,16,1]{2,1,0:T(8,128)S(1)}, f32[16,16,1]{2,1,0:T(8,128)S(1)}, u32[]{:S(2)}, u32[]{:S(2)}) collective-permute-start(f32[16,16,1]{2,1,0:T(8,128)S(1)} %get-tuple-element.51), channel_id=1, source_target_pairs={{128,0},{256,128},{384,256},{129,1},{257,129},{385,257},{130,2},{2... | collective-permute-start | bytes 3080 | tf_op jit(solution)/shard_map/ppermute | solution.py:22
  77.8 42.4 %slice-start = ((f32[8,64,256]{2,1,0:T(8,128)}), f32[8,64,64]{2,1,0:T(8,128)S(1)}, s32[]{:S(2)}) async-start(f32[8,64,256]{2,1,0:T(8,128)} %param.10), calls=%async_computation.3 | async-start | bytes 524288 | tf_op jit(solution)/shard_map/slice | solution.py:81
  77.8 4.5 collective-permute-start.14
  79.9 6.3 %collective-permute-start.15 = (f32[1,16,130]{2,1,0:T(8,128)S(1)}, f32[1,16,130]{2,1,0:T(8,128)S(1)}, u32[]{:S(2)}, u32[]{:S(2)}) collective-permute-start(f32[1,16,130]{2,1,0:T(8,128)S(1)} %get-tuple-element.39), channel_id=1, source_target_pairs={{0,8},{8,16},{16,24},{24,32},{32,40},{40,48},{48,56},{56,64},{64,7... | collective-permute-start | bytes 24968 | tf_op jit(solution)/shard_map/ppermute | solution.py:20
  86.3 7.4 %collective-permute-start.16 = (f32[18,1,130]{2,1,0:T(1,128)S(1)}, f32[18,1,130]{2,1,0:T(1,128)S(1)}, u32[]{:S(2)}, u32[]{:S(2)}) collective-permute-start(f32[18,1,130]{2,1,0:T(1,128)S(1)} %get-tuple-element.25), channel_id=1, source_target_pairs={{1,0},{2,1},{3,2},{4,3},{5,4},{6,5},{7,6},{9,8},{10,9},{11,10},{12... | collective-permute-start | bytes 28088 | tf_op jit(solution)/shard_map/ppermute | solution.py:22
  88.2 6.9 %collective-permute-start.17 = (f32[18,1,130]{2,1,0:T(1,128)S(1)}, f32[18,1,130]{2,1,0:T(1,128)S(1)}, u32[]{:S(2)}, u32[]{:S(2)}) collective-permute-start(f32[18,1,130]{2,1,0:T(1,128)S(1)} %get-tuple-element.26), channel_id=1, source_target_pairs={{0,1},{1,2},{2,3},{3,4},{4,5},{5,6},{6,7},{8,9},{9,10},{10,11},{11... | collective-permute-start | bytes 28088 | tf_op jit(solution)/shard_map/ppermute | solution.py:20
  95.6 5.2 collective-permute-start.18
  97.5 6.9 %collective-permute-start.19 = (f32[16,16,1]{2,1,0:T(8,128)S(1)}, f32[16,16,1]{2,1,0:T(8,128)S(1)}, u32[]{:S(2)}, u32[]{:S(2)}) collective-permute-start(f32[16,16,1]{2,1,0:T(8,128)S(1)} %get-tuple-element.49), channel_id=1, source_target_pairs={{128,0},{256,128},{384,256},{129,1},{257,129},{385,257},{130,2},{2... | collective-permute-start | bytes 3080 | tf_op jit(solution)/shard_map/ppermute | solution.py:22
  104.4 4.4 collective-permute-start.20
  106.4 6.3 %collective-permute-start.21 = (f32[1,16,130]{2,1,0:T(8,128)S(1)}, f32[1,16,130]{2,1,0:T(8,128)S(1)}, u32[]{:S(2)}, u32[]{:S(2)}) collective-permute-start(f32[1,16,130]{2,1,0:T(8,128)S(1)} %get-tuple-element.37), channel_id=1, source_target_pairs={{0,8},{8,16},{16,24},{24,32},{32,40},{40,48},{48,56},{56,64},{64,7... | collective-permute-start | bytes 24968 | tf_op jit(solution)/shard_map/ppermute | solution.py:20
  112.8 11.0 %collective-permute-start.22 = (f32[18,1,130]{2,1,0:T(1,128)S(1)}, f32[18,1,130]{2,1,0:T(1,128)S(1)}, u32[]{:S(2)}, u32[]{:S(2)}) collective-permute-start(f32[18,1,130]{2,1,0:T(1,128)S(1)} %get-tuple-element.23), channel_id=1, source_target_pairs={{1,0},{2,1},{3,2},{4,3},{5,4},{6,5},{7,6},{9,8},{10,9},{11,10},{12... | collective-permute-start | bytes 28088 | tf_op jit(solution)/shard_map/ppermute | solution.py:22
  114.7 9.1 %collective-permute-start.23 = (f32[18,1,130]{2,1,0:T(1,128)S(1)}, f32[18,1,130]{2,1,0:T(1,128)S(1)}, u32[]{:S(2)}, u32[]{:S(2)}) collective-permute-start(f32[18,1,130]{2,1,0:T(1,128)S(1)} %get-tuple-element.24), channel_id=1, source_target_pairs={{0,1},{1,2},{2,3},{3,4},{4,5},{5,6},{6,7},{8,9},{9,10},{10,11},{11... | collective-permute-start | bytes 28088 | tf_op jit(solution)/shard_map/ppermute | solution.py:20
  130.1 5.8 copy-start.7
  135.9 227.2 %all-gather.9.cloned.1.call-start = ((), (), s32[]{:S(2)}) async-start(), calls=%async_computation.1 | async-start | bytes 1050624 | tf_op jit(solution)/shard_map/all_gather | solution.py:84
  248.0 4.0 copy-start.2
  248.0 4.6 copy-start.4
  253.3 228.7 %all-gather.11.cloned.1.call-start = ((), (), s32[]{:S(2)}) async-start(), calls=%async_computation.2 | async-start | bytes 1050624 | tf_op jit(solution)/shard_map/all_gather | solution.py:84
  366.9 4.6 copy-start.6
  485.8 4.6 copy-start.5
  490.4 8.9 %copy-start = (f32[512]{0:T(512)}, f32[512]{0:T(512)S(1)}, u32[]{:S(2)}) copy-start(f32[512]{0:T(512)S(1)} %divide_add_fusion) | copy-start | bytes 6148
  494.3 5.0 collective-permute-start.24
  497.6 5.5 collective-permute-start.25
  503.4 4.3 collective-permute-start.26
  505.3 6.3 %collective-permute-start.27 = (f32[1,16,130]{2,1,0:T(8,128)S(1)}, f32[1,16,130]{2,1,0:T(8,128)S(1)}, u32[]{:S(2)}, u32[]{:S(2)}) collective-permute-start(f32[1,16,130]{2,1,0:T(8,128)S(1)} %get-tuple-element.35), channel_id=1, source_target_pairs={{0,8},{8,16},{16,24},{24,32},{32,40},{40,48},{48,56},{56,64},{64,7... | collective-permute-start | bytes 24968 | tf_op jit(solution)/shard_map/ppermute | solution.py:20
  511.7 7.1 %collective-permute-start.28 = (f32[18,1,130]{2,1,0:T(1,128)S(1)}, f32[18,1,130]{2,1,0:T(1,128)S(1)}, u32[]{:S(2)}, u32[]{:S(2)}) collective-permute-start(f32[18,1,130]{2,1,0:T(1,128)S(1)} %get-tuple-element.21), channel_id=1, source_target_pairs={{1,0},{2,1},{3,2},{4,3},{5,4},{6,5},{7,6},{9,8},{10,9},{11,10},{12... | collective-permute-start | bytes 28088 | tf_op jit(solution)/shard_map/ppermute | solution.py:22
  514.5 5.7 collective-permute-start.29
  520.7 5.9 %collective-permute-start.30 = (f32[16,16,1]{2,1,0:T(8,128)S(1)}, f32[16,16,1]{2,1,0:T(8,128)S(1)}, u32[]{:S(2)}, u32[]{:S(2)}) collective-permute-start(f32[16,16,1]{2,1,0:T(8,128)S(1)} %get-tuple-element.48), channel_id=1, source_target_pairs={{0,128},{128,256},{256,384},{1,129},{129,257},{257,385},{2,130},{1... | collective-permute-start | bytes 3080 | tf_op jit(solution)/shard_map/ppermute | solution.py:20
  524.1 6.9 %collective-permute-start.31 = (f32[16,16,1]{2,1,0:T(8,128)S(1)}, f32[16,16,1]{2,1,0:T(8,128)S(1)}, u32[]{:S(2)}, u32[]{:S(2)}) collective-permute-start(f32[16,16,1]{2,1,0:T(8,128)S(1)} %get-tuple-element.47), channel_id=1, source_target_pairs={{128,0},{256,128},{384,256},{129,1},{257,129},{385,257},{130,2},{2... | collective-permute-start | bytes 3080 | tf_op jit(solution)/shard_map/ppermute | solution.py:22
  531.0 4.3 collective-permute-start.32
  533.0 6.3 %collective-permute-start.33 = (f32[1,16,130]{2,1,0:T(8,128)S(1)}, f32[1,16,130]{2,1,0:T(8,128)S(1)}, u32[]{:S(2)}, u32[]{:S(2)}) collective-permute-start(f32[1,16,130]{2,1,0:T(8,128)S(1)} %get-tuple-element.33), channel_id=1, source_target_pairs={{0,8},{8,16},{16,24},{24,32},{32,40},{40,48},{48,56},{56,64},{64,7... | collective-permute-start | bytes 24968 | tf_op jit(solution)/shard_map/ppermute | solution.py:20
  539.4 7.4 %collective-permute-start.34 = (f32[18,1,130]{2,1,0:T(1,128)S(1)}, f32[18,1,130]{2,1,0:T(1,128)S(1)}, u32[]{:S(2)}, u32[]{:S(2)}) collective-permute-start(f32[18,1,130]{2,1,0:T(1,128)S(1)} %get-tuple-element.19), channel_id=1, source_target_pairs={{1,0},{2,1},{3,2},{4,3},{5,4},{6,5},{7,6},{9,8},{10,9},{11,10},{12... | collective-permute-start | bytes 28088 | tf_op jit(solution)/shard_map/ppermute | solution.py:22
  541.7 6.5 %collective-permute-start.35 = (f32[18,1,130]{2,1,0:T(1,128)S(1)}, f32[18,1,130]{2,1,0:T(1,128)S(1)}, u32[]{:S(2)}, u32[]{:S(2)}) collective-permute-start(f32[18,1,130]{2,1,0:T(1,128)S(1)} %get-tuple-element.20), channel_id=1, source_target_pairs={{0,1},{1,2},{2,3},{3,4},{4,5},{5,6},{6,7},{8,9},{9,10},{10,11},{11... | collective-permute-start | bytes 28088 | tf_op jit(solution)/shard_map/ppermute | solution.py:20
  548.7 5.6 collective-permute-start.36
  551.8 6.9 %collective-permute-start.37 = (f32[16,16,1]{2,1,0:T(8,128)S(1)}, f32[16,16,1]{2,1,0:T(8,128)S(1)}, u32[]{:S(2)}, u32[]{:S(2)}) collective-permute-start(f32[16,16,1]{2,1,0:T(8,128)S(1)} %get-tuple-element.45), channel_id=1, source_target_pairs={{128,0},{256,128},{384,256},{129,1},{257,129},{385,257},{130,2},{2... | collective-permute-start | bytes 3080 | tf_op jit(solution)/shard_map/ppermute | solution.py:22
  558.7 4.3 collective-permute-start.38
  560.6 6.3 %collective-permute-start.39 = (f32[1,16,130]{2,1,0:T(8,128)S(1)}, f32[1,16,130]{2,1,0:T(8,128)S(1)}, u32[]{:S(2)}, u32[]{:S(2)}) collective-permute-start(f32[1,16,130]{2,1,0:T(8,128)S(1)} %get-tuple-element.31), channel_id=1, source_target_pairs={{0,8},{8,16},{16,24},{24,32},{32,40},{40,48},{48,56},{56,64},{64,7... | collective-permute-start | bytes 24968 | tf_op jit(solution)/shard_map/ppermute | solution.py:20
  567.1 7.4 %collective-permute-start.40 = (f32[18,1,130]{2,1,0:T(1,128)S(1)}, f32[18,1,130]{2,1,0:T(1,128)S(1)}, u32[]{:S(2)}, u32[]{:S(2)}) collective-permute-start(f32[18,1,130]{2,1,0:T(1,128)S(1)} %get-tuple-element.17), channel_id=1, source_target_pairs={{1,0},{2,1},{3,2},{4,3},{5,4},{6,5},{7,6},{9,8},{10,9},{11,10},{12... | collective-permute-start | bytes 28088 | tf_op jit(solution)/shard_map/ppermute | solution.py:22
  569.0 6.9 %collective-permute-start.41 = (f32[18,1,130]{2,1,0:T(1,128)S(1)}, f32[18,1,130]{2,1,0:T(1,128)S(1)}, u32[]{:S(2)}, u32[]{:S(2)}) collective-permute-start(f32[18,1,130]{2,1,0:T(1,128)S(1)} %get-tuple-element.18), channel_id=1, source_target_pairs={{0,1},{1,2},{2,3},{3,4},{4,5},{5,6},{6,7},{8,9},{9,10},{10,11},{11... | collective-permute-start | bytes 28088 | tf_op jit(solution)/shard_map/ppermute | solution.py:20
Sparse Core Ops, SparseCore 0:
  136.0 108.1 all-gather.6
  253.4 109.6 all-gather.8
  372.3 109.6 all-gather.10
where the time goes:
time: 585 us; the launch traced here: 583 us
  waiting for transfers between devices  398 us (68%)
  starting transfers between devices  113 us (19%)
  local copies, waits for them, and re-layouts  32.4 us (6%)
  other arithmetic  24.2 us (4%)
  between operations  14.5 us (2%)
    all_gather x3, waiting for transfers between devices, local(): lax.all_gather(coarse_error, ('grp', 'gx', 'gy'), axis=0, tiled=True)  328 us
    ppermute x21, starting transfers between devices, padded_2(): lax.ppermute(tail, axis, [(i, (i + 1) % count) for i in range(ends)])  75 us
    ppermute x21, waiting for transfers between devices, padded_2(): lax.ppermute(tail, axis, [(i, (i + 1) % count) for i in range(ends)])  41.7 us
    ppermute x21, starting transfers between devices, padded_2(): lax.ppermute(head, axis, [((i + 1) % count, i) for i in range(ends)])  37.3 us
    ppermute x21, waiting for transfers between devices, padded_2(): lax.ppermute(head, axis, [((i + 1) % count, i) for i in range(ends)])  28.8 us
  transfers between devices with their start and end apart: 45, of which 28 were waited for; matrix products, arithmetic and copies ran while one was open for 1% of the time, Pallas kernels for 0%

commit v1 on v0

--- a/solution.py
+++ b/solution.py
@@ -81,7 +81,15 @@
     coarse_diag = jnp.diagonal(coarse_values[:, :, :64], axis1=1, axis2=2).reshape(-1)
     coarse_error = coarse_rhs / coarse_diag
     for sweep_number in range(CITER - 1):
-        gathered = lax.all_gather(coarse_error, ("grp", "gx", "gy"), axis=0, tiled=True)
+        gathered = jnp.concatenate(
+            lax.all_to_all(
+                jnp.stack([coarse_error] * lax.axis_size(("grp", "gx", "gy"))),
+                ("grp", "gx", "gy"),
+                0,
+                0,
+            ),
+            axis=0,
+        )
         blocks = gathered.reshape(-1, 64)[coarse_columns]
         blocks = blocks.reshape(blocks.shape[0], -1)
         applied = jnp.einsum(

time: 585 us -> 374 us (0.64)
  the two profiles are of different devices: /device:TPU:224 before, /device:TPU:32 now
where the time goes in v1:
time: 374 us; the launch traced here: 372 us
  starting transfers between devices  142 us (38%)
  waiting for transfers between devices  125 us (33%)
  blocking collectives  43.2 us (12%)
  local copies, waits for them, and re-layouts  36.2 us (10%)
  other arithmetic  22.2 us (6%)
    ppermute x21, starting transfers between devices, padded_2(): lax.ppermute(tail, axis, [(i, (i + 1) % count) for i in range(ends)])  72 us
    all_to_all x2, waiting for transfers between devices, local(): lax.all_to_all(jnp.stack([coarse_error] * lax.axis_size(('grp', 'gx', 'gy...  54.2 us
    all_to_all x1, blocking collectives, local(): lax.all_to_all(jnp.stack([coarse_error] * lax.axis_size(('grp', 'gx', 'gy...  43.2 us
    ppermute x21, waiting for transfers between devices, padded_2(): lax.ppermute(tail, axis, [(i, (i + 1) % count) for i in range(ends)])  42.1 us
    all_to_all x2, starting transfers between devices, local(): lax.all_to_all(jnp.stack([coarse_error] * lax.axis_size(('grp', 'gx', 'gy...  38.3 us
    ppermute x21, starting transfers between devices, padded_2(): lax.ppermute(head, axis, [((i + 1) % count, i) for i in range(ends)])  32 us
    ppermute x21, waiting for transfers between devices, padded_2(): lax.ppermute(head, axis, [((i + 1) % count, i) for i in range(ends)])  28.8 us
    all_to_all x3, other arithmetic, local(): lax.all_to_all(jnp.stack([coarse_error] * lax.axis_size(('grp', 'gx', 'gy...  11.4 us
  transfers between devices with their start and end apart: 44, of which 27 were waited for; matrix products, arithmetic and copies ran while one was open for 2% of the time, Pallas kernels for 0%

profile of v1, /device:TPU:32, one launch (start us, length us, event | category | flops | bytes accessed | tf_op | source)
XLA Modules:
  0.0 371.9 jit_solution(2371300776108533006)
XLA Ops:
  1.7 3.5 collective-permute-start
  8.0 4.1 %collective-permute-done.1 = f32[16,16,1]{2,1,0:T(8,128)S(1)} collective-permute-done((f32[16,16,1]{2,1,0:T(8,128)S(1)}, f32[16,16,1]{2,1,0:T(8,128)S(1)}, u32[]{:S(2)}, u32[]{:S(2)}) %collective-permute-start.1) | collective-permute-done | bytes 1056 | tf_op jit(solution)/shard_map/ppermute | solution.py:22
  12.9 1.9 collective-permute-start.2
  14.9 2.4 collective-permute-start.3
  17.3 3.8 %collective-permute-done.3 = f32[1,16,130]{2,1,0:T(8,128)S(1)} collective-permute-done((f32[1,16,130]{2,1,0:T(8,128)S(1)}, f32[1,16,130]{2,1,0:T(8,128)S(1)}, u32[]{:S(2)}, u32[]{:S(2)}) %collective-permute-start.3) | collective-permute-done | bytes 8352 | tf_op jit(solution)/shard_map/ppermute | solution.py:20
  23.5 4.9 %collective-permute-start.5 = (f32[18,1,130]{2,1,0:T(1,128)S(1)}, f32[18,1,130]{2,1,0:T(1,128)S(1)}, u32[]{:S(2)}, u32[]{:S(2)}) collective-permute-start(f32[18,1,130]{2,1,0:T(1,128)S(1)} %get-tuple-element.29), channel_id=1, source_target_pairs={{0,1},{1,2},{2,3},{3,4},{4,5},{5,6},{6,7},{8,9},{9,10},{10,11},{11... | collective-permute-start | bytes 28088 | tf_op jit(solution)/shard_map/ppermute | solution.py:20
  29.8 1.8 fusion.140
  31.8 3.4 collective-permute-start.6
  37.7 4.4 %collective-permute-done.7 = f32[16,16,1]{2,1,0:T(8,128)S(1)} collective-permute-done((f32[16,16,1]{2,1,0:T(8,128)S(1)}, f32[16,16,1]{2,1,0:T(8,128)S(1)}, u32[]{:S(2)}, u32[]{:S(2)}) %collective-permute-start.7) | collective-permute-done | bytes 1056 | tf_op jit(solution)/shard_map/ppermute | solution.py:22
  42.1 1.9 collective-permute-start.8
  44.0 2.4 collective-permute-start.9
  46.5 3.8 %collective-permute-done.9 = f32[1,16,130]{2,1,0:T(8,128)S(1)} collective-permute-done((f32[1,16,130]{2,1,0:T(8,128)S(1)}, f32[1,16,130]{2,1,0:T(8,128)S(1)}, u32[]{:S(2)}, u32[]{:S(2)}) %collective-permute-start.9) | collective-permute-done | bytes 8352 | tf_op jit(solution)/shard_map/ppermute | solution.py:20
  51.8 4.9 %collective-permute-start.11 = (f32[18,1,130]{2,1,0:T(1,128)S(1)}, f32[18,1,130]{2,1,0:T(1,128)S(1)}, u32[]{:S(2)}, u32[]{:S(2)}) collective-permute-start(f32[18,1,130]{2,1,0:T(1,128)S(1)} %get-tuple-element.28), channel_id=1, source_target_pairs={{0,1},{1,2},{2,3},{3,4},{4,5},{5,6},{6,7},{8,9},{9,10},{10,11},{11... | collective-permute-start | bytes 28088 | tf_op jit(solution)/shard_map/ppermute | solution.py:20
  58.6 3.1 collective-permute-start.12
  64.2 4.4 %collective-permute-done.13 = f32[16,16,1]{2,1,0:T(8,128)S(1)} collective-permute-done((f32[16,16,1]{2,1,0:T(8,128)S(1)}, f32[16,16,1]{2,1,0:T(8,128)S(1)}, u32[]{:S(2)}, u32[]{:S(2)}) %collective-permute-start.13) | collective-permute-done | bytes 1056 | tf_op jit(solution)/shard_map/ppermute | solution.py:22
  68.7 2.1 collective-permute-start.14
  70.7 2.4 collective-permute-start.15
  73.2 3.8 %collective-permute-done.15 = f32[1,16,130]{2,1,0:T(8,128)S(1)} collective-permute-done((f32[1,16,130]{2,1,0:T(8,128)S(1)}, f32[1,16,130]{2,1,0:T(8,128)S(1)}, u32[]{:S(2)}, u32[]{:S(2)}) %collective-permute-start.15) | collective-permute-done | bytes 8352 | tf_op jit(solution)/shard_map/ppermute | solution.py:20
  78.5 4.9 %collective-permute-start.17 = (f32[18,1,130]{2,1,0:T(1,128)S(1)}, f32[18,1,130]{2,1,0:T(1,128)S(1)}, u32[]{:S(2)}, u32[]{:S(2)}) collective-permute-start(f32[18,1,130]{2,1,0:T(1,128)S(1)} %get-tuple-element.26), channel_id=1, source_target_pairs={{0,1},{1,2},{2,3},{3,4},{4,5},{5,6},{6,7},{8,9},{9,10},{10,11},{11... | collective-permute-start | bytes 28088 | tf_op jit(solution)/shard_map/ppermute | solution.py:20
  85.3 1.9 collective-permute-start.18
  88.5 1.9 slice.324
  90.5 3.6 collective-permute-done.19
  94.2 1.9 collective-permute-start.20
  96.1 2.4 collective-permute-start.21
  98.5 3.8 %collective-permute-done.21 = f32[1,16,130]{2,1,0:T(8,128)S(1)} collective-permute-done((f32[1,16,130]{2,1,0:T(8,128)S(1)}, f32[1,16,130]{2,1,0:T(8,128)S(1)}, u32[]{:S(2)}, u32[]{:S(2)}) %collective-permute-start.21) | collective-permute-done | bytes 8352 | tf_op jit(solution)/shard_map/ppermute | solution.py:20
  103.8 6.1 %collective-permute-start.23 = (f32[18,1,130]{2,1,0:T(1,128)S(1)}, f32[18,1,130]{2,1,0:T(1,128)S(1)}, u32[]{:S(2)}, u32[]{:S(2)}) collective-permute-start(f32[18,1,130]{2,1,0:T(1,128)S(1)} %get-tuple-element.24), channel_id=1, source_target_pairs={{0,1},{1,2},{2,3},{3,4},{4,5},{5,6},{6,7},{8,9},{9,10},{10,11},{11... | collective-permute-start | bytes 28088 | tf_op jit(solution)/shard_map/ppermute | solution.py:20
  110.0 2.0 copy.270
  114.3 5.7 %reshape.99 = f32[4,4,4,4,32,4]{5,4,3,2,1,0:T(8,128)} reshape(f32[16,16,128]{2,1,0:T(8,128)S(1)} %fusion.70) | data formatting | bytes 262144 | tf_op jit(solution)/shard_map/reshape | solution.py:76
  120.0 2.6 reduce_sum.9
  122.7 2.4 scatter_custom_fusion
  126.7 22.3 %all-to-all-start = ((f32[512,1,512]{2,1,0:T(1,128)}), f32[512,1,512]{2,1,0:T(1,128)}, u32[]{:S(2)}, u32[]{:S(2)}) async-start(f32[512,1,512]{2,1,0:T(1,128)} %stack.6), calls=%async_computation | async-start | bytes 2097152 | tf_op jit(solution)/shard_map/all_to_all | solution.py:85
  149.2 27.0 %all-to-all-done = f32[512,1,512]{2,1,0:T(1,128)} async-done(((f32[512,1,512]{2,1,0:T(1,128)}), f32[512,1,512]{2,1,0:T(1,128)}, u32[]{:S(2)}, u32[]{:S(2)}) %all-to-all-start) | async-done | bytes 1048608 | tf_op jit(solution)/shard_map/all_to_all | solution.py:85
  176.2 3.8 %reduce = f32[512,512]{1,0:T(8,128)S(1)} reduce(f32[512,1,512]{2,1,0:T(1,128)} %all-to-all-done, f32[]{:T(128)} %constant.34), dimensions={1}, to_apply=%all_to_all.12.reduce_sub_computation | reduce | bytes 2097156 | tf_op jit(solution)/shard_map/all_to_all | solution.py:85
  180.0 1.8 reshape_reshape.9
  181.8 2.2 gather_fusion.1
  185.2 43.2 %all_to_all.18 = f32[512,1,512]{2,1,0:T(1,128)} all-to-all(f32[512,1,512]{2,1,0:T(1,128)S(1)} %stack.7), channel_id=1, replica_groups=mesh['grp'=4,'gx'=16,'gy'=8] {'grp','gx','gy'}, dimensions={0} | all-to-all | bytes 2097152 | tf_op jit(solution)/shard_map/all_to_all | solution.py:85
  228.4 3.8 %reduce.1 = f32[512,512]{1,0:T(8,128)S(1)} reduce(f32[512,1,512]{2,1,0:T(1,128)} %all_to_all.18, f32[]{:T(128)} %constant.34), dimensions={1}, to_apply=%all_to_all.13.reduce_sub_computation | reduce | bytes 2097156 | tf_op jit(solution)/shard_map/all_to_all | solution.py:85
  232.2 1.8 reshape_reshape.10
  234.0 2.2 gather_fusion.2
  236.9 1.6 stack.8
  238.4 15.9 %all-to-all-start.2 = ((f32[512,1,512]{2,1,0:T(1,128)}), f32[512,1,512]{2,1,0:T(1,128)}, u32[]{:S(2)}, u32[]{:S(2)}) async-start(f32[512,1,512]{2,1,0:T(1,128)} %stack.8), calls=%async_computation.2 | async-start | bytes 2097152 | tf_op jit(solution)/shard_map/all_to_all | solution.py:85
  254.4 27.2 %all-to-all-done.2 = f32[512,1,512]{2,1,0:T(1,128)} async-done(((f32[512,1,512]{2,1,0:T(1,128)}), f32[512,1,512]{2,1,0:T(1,128)}, u32[]{:S(2)}, u32[]{:S(2)}) %all-to-all-start.2) | async-done | bytes 1048608 | tf_op jit(solution)/shard_map/all_to_all | solution.py:85
  281.6 3.8 %reduce.2 = f32[512,512]{1,0:T(8,128)S(1)} reduce(f32[512,1,512]{2,1,0:T(1,128)} %all-to-all-done.2, f32[]{:T(128)} %constant.34), dimensions={1}, to_apply=%all_to_all.14.reduce_sub_computation | reduce | bytes 2097156 | tf_op jit(solution)/shard_map/all_to_all | solution.py:85
  285.4 1.8 reshape_reshape.11
  287.1 2.2 gather_fusion.3
  290.0 3.5 gather_fusion.4
  293.9 2.5 collective-permute-start.24
  298.3 3.6 collective-permute-done.25
  302.2 2.3 collective-permute-start.26
  304.5 2.1 collective-permute-start.27
  306.5 4.2 %collective-permute-done.27 = f32[1,16,130]{2,1,0:T(8,128)S(1)} collective-permute-done((f32[1,16,130]{2,1,0:T(8,128)S(1)}, f32[1,16,130]{2,1,0:T(8,128)S(1)}, u32[]{:S(2)}, u32[]{:S(2)}) %collective-permute-start.27) | collective-permute-done | bytes 8352 | tf_op jit(solution)/shard_map/ppermute | solution.py:20
  312.2 4.5 %collective-permute-start.29 = (f32[18,1,130]{2,1,0:T(1,128)S(1)}, f32[18,1,130]{2,1,0:T(1,128)S(1)}, u32[]{:S(2)}, u32[]{:S(2)}) collective-permute-start(f32[18,1,130]{2,1,0:T(1,128)S(1)} %get-tuple-element.22), channel_id=1, source_target_pairs={{0,1},{1,2},{2,3},{3,4},{4,5},{5,6},{6,7},{8,9},{9,10},{10,11},{11... | collective-permute-start | bytes 28088 | tf_op jit(solution)/shard_map/ppermute | solution.py:20
  318.7 2.6 collective-permute-start.30
  323.8 4.4 %collective-permute-done.31 = f32[16,16,1]{2,1,0:T(8,128)S(1)} collective-permute-done((f32[16,16,1]{2,1,0:T(8,128)S(1)}, f32[16,16,1]{2,1,0:T(8,128)S(1)}, u32[]{:S(2)}, u32[]{:S(2)}) %collective-permute-start.31) | collective-permute-done | bytes 1056 | tf_op jit(solution)/shard_map/ppermute | solution.py:22
  328.2 1.9 collective-permute-start.32
  330.1 2.4 collective-permute-start.33
  332.6 3.8 %collective-permute-done.33 = f32[1,16,130]{2,1,0:T(8,128)S(1)} collective-permute-done((f32[1,16,130]{2,1,0:T(8,128)S(1)}, f32[1,16,130]{2,1,0:T(8,128)S(1)}, u32[]{:S(2)}, u32[]{:S(2)}) %collective-permute-start.33) | collective-permute-done | bytes 8352 | tf_op jit(solution)/shard_map/ppermute | solution.py:20
  337.9 4.8 %collective-permute-start.35 = (f32[18,1,130]{2,1,0:T(1,128)S(1)}, f32[18,1,130]{2,1,0:T(1,128)S(1)}, u32[]{:S(2)}, u32[]{:S(2)}) collective-permute-start(f32[18,1,130]{2,1,0:T(1,128)S(1)} %get-tuple-element.20), channel_id=1, source_target_pairs={{0,1},{1,2},{2,3},{3,4},{4,5},{5,6},{6,7},{8,9},{9,10},{10,11},{11... | collective-permute-start | bytes 28088 | tf_op jit(solution)/shard_map/ppermute | solution.py:20
  344.6 3.4 collective-permute-start.36
  350.5 4.4 %collective-permute-done.37 = f32[16,16,1]{2,1,0:T(8,128)S(1)} collective-permute-done((f32[16,16,1]{2,1,0:T(8,128)S(1)}, f32[16,16,1]{2,1,0:T(8,128)S(1)}, u32[]{:S(2)}, u32[]{:S(2)}) %collective-permute-start.37) | collective-permute-done | bytes 1056 | tf_op jit(solution)/shard_map/ppermute | solution.py:22
  355.0 1.9 collective-permute-start.38
  356.9 2.4 collective-permute-start.39
  359.3 3.8 %collective-permute-done.39 = f32[1,16,130]{2,1,0:T(8,128)S(1)} collective-permute-done((f32[1,16,130]{2,1,0:T(8,128)S(1)}, f32[1,16,130]{2,1,0:T(8,128)S(1)}, u32[]{:S(2)}, u32[]{:S(2)}) %collective-permute-start.39) | collective-permute-done | bytes 8352 | tf_op jit(solution)/shard_map/ppermute | solution.py:20
  364.6 4.8 %collective-permute-start.41 = (f32[18,1,130]{2,1,0:T(1,128)S(1)}, f32[18,1,130]{2,1,0:T(1,128)S(1)}, u32[]{:S(2)}, u32[]{:S(2)}) collective-permute-start(f32[18,1,130]{2,1,0:T(1,128)S(1)} %get-tuple-element.18), channel_id=1, source_target_pairs={{0,1},{1,2},{2,3},{3,4},{4,5},{5,6},{6,7},{8,9},{9,10},{10,11},{11... | collective-permute-start | bytes 28088 | tf_op jit(solution)/shard_map/ppermute | solution.py:20
  (117 shorter events, 48.2 us)
Async XLA Ops:
  1.7 56.4 %copy-start.1 = (f32[16,16,128]{2,1,0:T(8,128)S(1)}, f32[16,16,128]{2,1,0:T(8,128)}, u32[]{:S(2)}) copy-start(f32[16,16,128]{2,1,0:T(8,128)} %param.8) | copy-start | bytes 393220
  1.7 56.4 %copy-start.3 = (f32[16,16,128]{2,1,0:T(8,128)S(1)}, f32[16,16,128]{2,1,0:T(8,128)}, u32[]{:S(2)}) copy-start(f32[16,16,128]{2,1,0:T(8,128)} %param.6) | copy-start | bytes 393220
  1.7 6.3 %collective-permute-start = (f32[16,16,1]{2,1,0:T(8,128)S(1)}, f32[16,16,1]{2,1,0:T(8,128)S(1)}, u32[]{:S(2)}, u32[]{:S(2)}) collective-permute-start(f32[16,16,1]{2,1,0:T(8,128)S(1)} %get-tuple-element.55), channel_id=1, source_target_pairs={{0,128},{128,256},{256,384},{1,129},{129,257},{257,385},{2,130},{1... | collective-permute-start | bytes 3080 | tf_op jit(solution)/shard_map/ppermute | solution.py:20
  5.3 6.9 %collective-permute-start.1 = (f32[16,16,1]{2,1,0:T(8,128)S(1)}, f32[16,16,1]{2,1,0:T(8,128)S(1)}, u32[]{:S(2)}, u32[]{:S(2)}) collective-permute-start(f32[16,16,1]{2,1,0:T(8,128)S(1)} %get-tuple-element.56), channel_id=1, source_target_pairs={{128,0},{256,128},{384,256},{129,1},{257,129},{385,257},{130,2},{2... | collective-permute-start | bytes 3080 | tf_op jit(solution)/shard_map/ppermute | solution.py:22
  12.9 4.3 %collective-permute-start.2 = (f32[1,16,130]{2,1,0:T(8,128)S(1)}, f32[1,16,130]{2,1,0:T(8,128)S(1)}, u32[]{:S(2)}, u32[]{:S(2)}) collective-permute-start(f32[1,16,130]{2,1,0:T(8,128)S(1)} %get-tuple-element.44), channel_id=1, source_target_pairs={{8,0},{16,8},{24,16},{32,24},{40,32},{48,40},{56,48},{64,56},{72,6... | collective-permute-start | bytes 24968 | tf_op jit(solution)/shard_map/ppermute | solution.py:22
  14.9 6.3 %collective-permute-start.3 = (f32[1,16,130]{2,1,0:T(8,128)S(1)}, f32[1,16,130]{2,1,0:T(8,128)S(1)}, u32[]{:S(2)}, u32[]{:S(2)}) collective-permute-start(f32[1,16,130]{2,1,0:T(8,128)S(1)} %get-tuple-element.43), channel_id=1, source_target_pairs={{0,8},{8,16},{16,24},{24,32},{32,40},{40,48},{48,56},{56,64},{64,7... | collective-permute-start | bytes 24968 | tf_op jit(solution)/shard_map/ppermute | solution.py:20
  22.2 6.2 %collective-permute-start.4 = (f32[18,1,130]{2,1,0:T(1,128)S(1)}, f32[18,1,130]{2,1,0:T(1,128)S(1)}, u32[]{:S(2)}, u32[]{:S(2)}) collective-permute-start(f32[18,1,130]{2,1,0:T(1,128)S(1)} %get-tuple-element.30), channel_id=1, source_target_pairs={{1,0},{2,1},{3,2},{4,3},{5,4},{6,5},{7,6},{9,8},{10,9},{11,10},{12... | collective-permute-start | bytes 28088 | tf_op jit(solution)/shard_map/ppermute | solution.py:22
  23.5 6.4 %collective-permute-start.5 = (f32[18,1,130]{2,1,0:T(1,128)S(1)}, f32[18,1,130]{2,1,0:T(1,128)S(1)}, u32[]{:S(2)}, u32[]{:S(2)}) collective-permute-start(f32[18,1,130]{2,1,0:T(1,128)S(1)} %get-tuple-element.29), channel_id=1, source_target_pairs={{0,1},{1,2},{2,3},{3,4},{4,5},{5,6},{6,7},{8,9},{9,10},{10,11},{11... | collective-permute-start | bytes 28088 | tf_op jit(solution)/shard_map/ppermute | solution.py:20
  31.8 5.9 %collective-permute-start.6 = (f32[16,16,1]{2,1,0:T(8,128)S(1)}, f32[16,16,1]{2,1,0:T(8,128)S(1)}, u32[]{:S(2)}, u32[]{:S(2)}) collective-permute-start(f32[16,16,1]{2,1,0:T(8,128)S(1)} %get-tuple-element.54), channel_id=1, source_target_pairs={{0,128},{128,256},{256,384},{1,129},{129,257},{257,385},{2,130},{1... | collective-permute-start | bytes 3080 | tf_op jit(solution)/shard_map/ppermute | solution.py:20
  35.2 6.9 %collective-permute-start.7 = (f32[16,16,1]{2,1,0:T(8,128)S(1)}, f32[16,16,1]{2,1,0:T(8,128)S(1)}, u32[]{:S(2)}, u32[]{:S(2)}) collective-permute-start(f32[16,16,1]{2,1,0:T(8,128)S(1)} %get-tuple-element.53), channel_id=1, source_target_pairs={{128,0},{256,128},{384,256},{129,1},{257,129},{385,257},{130,2},{2... | collective-permute-start | bytes 3080 | tf_op jit(solution)/shard_map/ppermute | solution.py:22
  42.1 4.3 %collective-permute-start.8 = (f32[1,16,130]{2,1,0:T(8,128)S(1)}, f32[1,16,130]{2,1,0:T(8,128)S(1)}, u32[]{:S(2)}, u32[]{:S(2)}) collective-permute-start(f32[1,16,130]{2,1,0:T(8,128)S(1)} %get-tuple-element.42), channel_id=1, source_target_pairs={{8,0},{16,8},{24,16},{32,24},{40,32},{48,40},{56,48},{64,56},{72,6... | collective-permute-start | bytes 24968 | tf_op jit(solution)/shard_map/ppermute | solution.py:22
  44.0 6.3 %collective-permute-start.9 = (f32[1,16,130]{2,1,0:T(8,128)S(1)}, f32[1,16,130]{2,1,0:T(8,128)S(1)}, u32[]{:S(2)}, u32[]{:S(2)}) collective-permute-start(f32[1,16,130]{2,1,0:T(8,128)S(1)} %get-tuple-element.41), channel_id=1, source_target_pairs={{0,8},{8,16},{16,24},{24,32},{32,40},{40,48},{48,56},{56,64},{64,7... | collective-permute-start | bytes 24968 | tf_op jit(solution)/shard_map/ppermute | solution.py:20
  50.5 6.2 %collective-permute-start.10 = (f32[18,1,130]{2,1,0:T(1,128)S(1)}, f32[18,1,130]{2,1,0:T(1,128)S(1)}, u32[]{:S(2)}, u32[]{:S(2)}) collective-permute-start(f32[18,1,130]{2,1,0:T(1,128)S(1)} %get-tuple-element.27), channel_id=1, source_target_pairs={{1,0},{2,1},{3,2},{4,3},{5,4},{6,5},{7,6},{9,8},{10,9},{11,10},{12... | collective-permute-start | bytes 28088 | tf_op jit(solution)/shard_map/ppermute | solution.py:22
  51.8 6.4 %collective-permute-start.11 = (f32[18,1,130]{2,1,0:T(1,128)S(1)}, f32[18,1,130]{2,1,0:T(1,128)S(1)}, u32[]{:S(2)}, u32[]{:S(2)}) collective-permute-start(f32[18,1,130]{2,1,0:T(1,128)S(1)} %get-tuple-element.28), channel_id=1, source_target_pairs={{0,1},{1,2},{2,3},{3,4},{4,5},{5,6},{6,7},{8,9},{9,10},{10,11},{11... | collective-permute-start | bytes 28088 | tf_op jit(solution)/shard_map/ppermute | solution.py:20
  58.6 5.6 %collective-permute-start.12 = (f32[16,16,1]{2,1,0:T(8,128)S(1)}, f32[16,16,1]{2,1,0:T(8,128)S(1)}, u32[]{:S(2)}, u32[]{:S(2)}) collective-permute-start(f32[16,16,1]{2,1,0:T(8,128)S(1)} %get-tuple-element.52), channel_id=1, source_target_pairs={{0,128},{128,256},{256,384},{1,129},{129,257},{257,385},{2,130},{1... | collective-permute-start | bytes 3080 | tf_op jit(solution)/shard_map/ppermute | solution.py:20
  61.7 6.9 %collective-permute-start.13 = (f32[16,16,1]{2,1,0:T(8,128)S(1)}, f32[16,16,1]{2,1,0:T(8,128)S(1)}, u32[]{:S(2)}, u32[]{:S(2)}) collective-permute-start(f32[16,16,1]{2,1,0:T(8,128)S(1)} %get-tuple-element.51), channel_id=1, source_target_pairs={{128,0},{256,128},{384,256},{129,1},{257,129},{385,257},{130,2},{2... | collective-permute-start | bytes 3080 | tf_op jit(solution)/shard_map/ppermute | solution.py:22
  68.7 41.3 %slice-start = ((f32[8,64,256]{2,1,0:T(8,128)}), f32[8,64,64]{2,1,0:T(8,128)S(1)}, s32[]{:S(2)}) async-start(f32[8,64,256]{2,1,0:T(8,128)} %param.10), calls=%async_computation.3 | async-start | bytes 524288 | tf_op jit(solution)/shard_map/slice | solution.py:81
  68.7 4.5 %collective-permute-start.14 = (f32[1,16,130]{2,1,0:T(8,128)S(1)}, f32[1,16,130]{2,1,0:T(8,128)S(1)}, u32[]{:S(2)}, u32[]{:S(2)}) collective-permute-start(f32[1,16,130]{2,1,0:T(8,128)S(1)} %get-tuple-element.40), channel_id=1, source_target_pairs={{8,0},{16,8},{24,16},{32,24},{40,32},{48,40},{56,48},{64,56},{72,6... | collective-permute-start | bytes 24968 | tf_op jit(solution)/shard_map/ppermute | solution.py:22
  70.7 6.3 %collective-permute-start.15 = (f32[1,16,130]{2,1,0:T(8,128)S(1)}, f32[1,16,130]{2,1,0:T(8,128)S(1)}, u32[]{:S(2)}, u32[]{:S(2)}) collective-permute-start(f32[1,16,130]{2,1,0:T(8,128)S(1)} %get-tuple-element.39), channel_id=1, source_target_pairs={{0,8},{8,16},{16,24},{24,32},{32,40},{40,48},{48,56},{56,64},{64,7... | collective-permute-start | bytes 24968 | tf_op jit(solution)/shard_map/ppermute | solution.py:20
  77.2 6.2 %collective-permute-start.16 = (f32[18,1,130]{2,1,0:T(1,128)S(1)}, f32[18,1,130]{2,1,0:T(1,128)S(1)}, u32[]{:S(2)}, u32[]{:S(2)}) collective-permute-start(f32[18,1,130]{2,1,0:T(1,128)S(1)} %get-tuple-element.25), channel_id=1, source_target_pairs={{1,0},{2,1},{3,2},{4,3},{5,4},{6,5},{7,6},{9,8},{10,9},{11,10},{12... | collective-permute-start | bytes 28088 | tf_op jit(solution)/shard_map/ppermute | solution.py:22
  78.5 6.4 %collective-permute-start.17 = (f32[18,1,130]{2,1,0:T(1,128)S(1)}, f32[18,1,130]{2,1,0:T(1,128)S(1)}, u32[]{:S(2)}, u32[]{:S(2)}) collective-permute-start(f32[18,1,130]{2,1,0:T(1,128)S(1)} %get-tuple-element.26), channel_id=1, source_target_pairs={{0,1},{1,2},{2,3},{3,4},{4,5},{5,6},{6,7},{8,9},{9,10},{10,11},{11... | collective-permute-start | bytes 28088 | tf_op jit(solution)/shard_map/ppermute | solution.py:20
  85.3 5.2 %collective-permute-start.18 = (f32[16,16,1]{2,1,0:T(8,128)S(1)}, f32[16,16,1]{2,1,0:T(8,128)S(1)}, u32[]{:S(2)}, u32[]{:S(2)}) collective-permute-start(f32[16,16,1]{2,1,0:T(8,128)S(1)} %get-tuple-element.50), channel_id=1, source_target_pairs={{0,128},{128,256},{256,384},{1,129},{129,257},{257,385},{2,130},{1... | collective-permute-start | bytes 3080 | tf_op jit(solution)/shard_map/ppermute | solution.py:20
  87.2 6.9 %collective-permute-start.19 = (f32[16,16,1]{2,1,0:T(8,128)S(1)}, f32[16,16,1]{2,1,0:T(8,128)S(1)}, u32[]{:S(2)}, u32[]{:S(2)}) collective-permute-start(f32[16,16,1]{2,1,0:T(8,128)S(1)} %get-tuple-element.49), channel_id=1, source_target_pairs={{128,0},{256,128},{384,256},{129,1},{257,129},{385,257},{130,2},{2... | collective-permute-start | bytes 3080 | tf_op jit(solution)/shard_map/ppermute | solution.py:22
  94.2 4.4 %collective-permute-start.20 = (f32[1,16,130]{2,1,0:T(8,128)S(1)}, f32[1,16,130]{2,1,0:T(8,128)S(1)}, u32[]{:S(2)}, u32[]{:S(2)}) collective-permute-start(f32[1,16,130]{2,1,0:T(8,128)S(1)} %get-tuple-element.38), channel_id=1, source_target_pairs={{8,0},{16,8},{24,16},{32,24},{40,32},{48,40},{56,48},{64,56},{72,6... | collective-permute-start | bytes 24968 | tf_op jit(solution)/shard_map/ppermute | solution.py:22
  96.1 6.3 %collective-permute-start.21 = (f32[1,16,130]{2,1,0:T(8,128)S(1)}, f32[1,16,130]{2,1,0:T(8,128)S(1)}, u32[]{:S(2)}, u32[]{:S(2)}) collective-permute-start(f32[1,16,130]{2,1,0:T(8,128)S(1)} %get-tuple-element.37), channel_id=1, source_target_pairs={{0,8},{8,16},{16,24},{24,32},{32,40},{40,48},{48,56},{56,64},{64,7... | collective-permute-start | bytes 24968 | tf_op jit(solution)/shard_map/ppermute | solution.py:20
  102.5 11.1 %collective-permute-start.22 = (f32[18,1,130]{2,1,0:T(1,128)S(1)}, f32[18,1,130]{2,1,0:T(1,128)S(1)}, u32[]{:S(2)}, u32[]{:S(2)}) collective-permute-start(f32[18,1,130]{2,1,0:T(1,128)S(1)} %get-tuple-element.23), channel_id=1, source_target_pairs={{1,0},{2,1},{3,2},{4,3},{5,4},{6,5},{7,6},{9,8},{10,9},{11,10},{12... | collective-permute-start | bytes 28088 | tf_op jit(solution)/shard_map/ppermute | solution.py:22
  103.8 9.8 %collective-permute-start.23 = (f32[18,1,130]{2,1,0:T(1,128)S(1)}, f32[18,1,130]{2,1,0:T(1,128)S(1)}, u32[]{:S(2)}, u32[]{:S(2)}) collective-permute-start(f32[18,1,130]{2,1,0:T(1,128)S(1)} %get-tuple-element.24), channel_id=1, source_target_pairs={{0,1},{1,2},{2,3},{3,4},{4,5},{5,6},{6,7},{8,9},{9,10},{10,11},{11... | collective-permute-start | bytes 28088 | tf_op jit(solution)/shard_map/ppermute | solution.py:20
  122.6 26.4 %copy-start.4 = (s32[8,4]{0,1:T(4,128)S(1)}, s32[8,4]{0,1:T(4,128)}, u32[]{:S(2)}) copy-start(s32[8,4]{0,1:T(4,128)} %param.11) | copy-start | bytes 388
  126.7 49.5 %all-to-all-start = ((f32[512,1,512]{2,1,0:T(1,128)}), f32[512,1,512]{2,1,0:T(1,128)}, u32[]{:S(2)}, u32[]{:S(2)}) async-start(f32[512,1,512]{2,1,0:T(1,128)} %stack.6), calls=%async_computation | async-start | bytes 2097152 | tf_op jit(solution)/shard_map/all_to_all | solution.py:85
  180.0 4.0 %copy-start.2 = (f32[8,64,256]{2,1,0:T(8,128)S(1)}, f32[8,64,256]{2,1,0:T(8,128)}, u32[]{:S(2)}) copy-start(f32[8,64,256]{2,1,0:T(8,128)} %param.10) | copy-start | bytes 1572868
  238.4 43.1 %all-to-all-start.2 = ((f32[512,1,512]{2,1,0:T(1,128)}), f32[512,1,512]{2,1,0:T(1,128)}, u32[]{:S(2)}, u32[]{:S(2)}) async-start(f32[512,1,512]{2,1,0:T(1,128)} %stack.8), calls=%async_computation.2 | async-start | bytes 2097152 | tf_op jit(solution)/shard_map/all_to_all | solution.py:85
  290.0 8.2 %copy-start = (f32[512]{0:T(512)}, f32[512]{0:T(512)S(1)}, u32[]{:S(2)}) copy-start(f32[512]{0:T(512)S(1)} %divide_add_fusion) | copy-start | bytes 6148
  293.9 4.2 %collective-permute-start.24 = (f32[16,16,1]{1,0,2:T(8,128)S(1)}, f32[16,16,1]{1,0,2:T(8,128)S(1)}, u32[]{:S(2)}, u32[]{:S(2)}) collective-permute-start(f32[16,16,1]{1,0,2:T(8,128)S(1)} %get-tuple-element.16), channel_id=1, source_target_pairs={{0,128},{128,256},{256,384},{1,129},{129,257},{257,385},{2,130},{1... | collective-permute-start | bytes 3080 | tf_op jit(solution)/shard_map/ppermute | solution.py:20
  296.4 5.5 %collective-permute-start.25 = (f32[16,16,1]{1,0,2:T(8,128)S(1)}, f32[16,16,1]{1,0,2:T(8,128)S(1)}, u32[]{:S(2)}, u32[]{:S(2)}) collective-permute-start(f32[16,16,1]{1,0,2:T(8,128)S(1)} %get-tuple-element.15), channel_id=1, source_target_pairs={{128,0},{256,128},{384,256},{129,1},{257,129},{385,257},{130,2},{2... | collective-permute-start | bytes 3080 | tf_op jit(solution)/shard_map/ppermute | solution.py:22
  302.2 4.3 %collective-permute-start.26 = (f32[1,16,130]{2,1,0:T(8,128)S(1)}, f32[1,16,130]{2,1,0:T(8,128)S(1)}, u32[]{:S(2)}, u32[]{:S(2)}) collective-permute-start(f32[1,16,130]{2,1,0:T(8,128)S(1)} %get-tuple-element.36), channel_id=1, source_target_pairs={{8,0},{16,8},{24,16},{32,24},{40,32},{48,40},{56,48},{64,56},{72,6... | collective-permute-start | bytes 24968 | tf_op jit(solution)/shard_map/ppermute | solution.py:22
  304.5 6.3 %collective-permute-start.27 = (f32[1,16,130]{2,1,0:T(8,128)S(1)}, f32[1,16,130]{2,1,0:T(8,128)S(1)}, u32[]{:S(2)}, u32[]{:S(2)}) collective-permute-start(f32[1,16,130]{2,1,0:T(8,128)S(1)} %get-tuple-element.35), channel_id=1, source_target_pairs={{0,8},{8,16},{16,24},{24,32},{32,40},{40,48},{48,56},{56,64},{64,7... | collective-permute-start | bytes 24968 | tf_op jit(solution)/shard_map/ppermute | solution.py:20
  310.9 5.9 %collective-permute-start.28 = (f32[18,1,130]{2,1,0:T(1,128)S(1)}, f32[18,1,130]{2,1,0:T(1,128)S(1)}, u32[]{:S(2)}, u32[]{:S(2)}) collective-permute-start(f32[18,1,130]{2,1,0:T(1,128)S(1)} %get-tuple-element.21), channel_id=1, source_target_pairs={{1,0},{2,1},{3,2},{4,3},{5,4},{6,5},{7,6},{9,8},{10,9},{11,10},{12... | collective-permute-start | bytes 28088 | tf_op jit(solution)/shard_map/ppermute | solution.py:22
  312.2 6.0 %collective-permute-start.29 = (f32[18,1,130]{2,1,0:T(1,128)S(1)}, f32[18,1,130]{2,1,0:T(1,128)S(1)}, u32[]{:S(2)}, u32[]{:S(2)}) collective-permute-start(f32[18,1,130]{2,1,0:T(1,128)S(1)} %get-tuple-element.22), channel_id=1, source_target_pairs={{0,1},{1,2},{2,3},{3,4},{4,5},{5,6},{6,7},{8,9},{9,10},{10,11},{11... | collective-permute-start | bytes 28088 | tf_op jit(solution)/shard_map/ppermute | solution.py:20
  318.7 5.1 %collective-permute-start.30 = (f32[16,16,1]{2,1,0:T(8,128)S(1)}, f32[16,16,1]{2,1,0:T(8,128)S(1)}, u32[]{:S(2)}, u32[]{:S(2)}) collective-permute-start(f32[16,16,1]{2,1,0:T(8,128)S(1)} %get-tuple-element.48), channel_id=1, source_target_pairs={{0,128},{128,256},{256,384},{1,129},{129,257},{257,385},{2,130},{1... | collective-permute-start | bytes 3080 | tf_op jit(solution)/shard_map/ppermute | solution.py:20
  321.3 6.9 %collective-permute-start.31 = (f32[16,16,1]{2,1,0:T(8,128)S(1)}, f32[16,16,1]{2,1,0:T(8,128)S(1)}, u32[]{:S(2)}, u32[]{:S(2)}) collective-permute-start(f32[16,16,1]{2,1,0:T(8,128)S(1)} %get-tuple-element.47), channel_id=1, source_target_pairs={{128,0},{256,128},{384,256},{129,1},{257,129},{385,257},{130,2},{2... | collective-permute-start | bytes 3080 | tf_op jit(solution)/shard_map/ppermute | solution.py:22
  328.2 4.3 %collective-permute-start.32 = (f32[1,16,130]{2,1,0:T(8,128)S(1)}, f32[1,16,130]{2,1,0:T(8,128)S(1)}, u32[]{:S(2)}, u32[]{:S(2)}) collective-permute-start(f32[1,16,130]{2,1,0:T(8,128)S(1)} %get-tuple-element.34), channel_id=1, source_target_pairs={{8,0},{16,8},{24,16},{32,24},{40,32},{48,40},{56,48},{64,56},{72,6... | collective-permute-start | bytes 24968 | tf_op jit(solution)/shard_map/ppermute | solution.py:22
  330.1 6.3 %collective-permute-start.33 = (f32[1,16,130]{2,1,0:T(8,128)S(1)}, f32[1,16,130]{2,1,0:T(8,128)S(1)}, u32[]{:S(2)}, u32[]{:S(2)}) collective-permute-start(f32[1,16,130]{2,1,0:T(8,128)S(1)} %get-tuple-element.33), channel_id=1, source_target_pairs={{0,8},{8,16},{16,24},{24,32},{32,40},{40,48},{48,56},{56,64},{64,7... | collective-permute-start | bytes 24968 | tf_op jit(solution)/shard_map/ppermute | solution.py:20
  336.6 6.1 %collective-permute-start.34 = (f32[18,1,130]{2,1,0:T(1,128)S(1)}, f32[18,1,130]{2,1,0:T(1,128)S(1)}, u32[]{:S(2)}, u32[]{:S(2)}) collective-permute-start(f32[18,1,130]{2,1,0:T(1,128)S(1)} %get-tuple-element.19), channel_id=1, source_target_pairs={{1,0},{2,1},{3,2},{4,3},{5,4},{6,5},{7,6},{9,8},{10,9},{11,10},{12... | collective-permute-start | bytes 28088 | tf_op jit(solution)/shard_map/ppermute | solution.py:22
  337.9 6.3 %collective-permute-start.35 = (f32[18,1,130]{2,1,0:T(1,128)S(1)}, f32[18,1,130]{2,1,0:T(1,128)S(1)}, u32[]{:S(2)}, u32[]{:S(2)}) collective-permute-start(f32[18,1,130]{2,1,0:T(1,128)S(1)} %get-tuple-element.20), channel_id=1, source_target_pairs={{0,1},{1,2},{2,3},{3,4},{4,5},{5,6},{6,7},{8,9},{9,10},{10,11},{11... | collective-permute-start | bytes 28088 | tf_op jit(solution)/shard_map/ppermute | solution.py:20
  344.6 5.9 %collective-permute-start.36 = (f32[16,16,1]{2,1,0:T(8,128)S(1)}, f32[16,16,1]{2,1,0:T(8,128)S(1)}, u32[]{:S(2)}, u32[]{:S(2)}) collective-permute-start(f32[16,16,1]{2,1,0:T(8,128)S(1)} %get-tuple-element.46), channel_id=1, source_target_pairs={{0,128},{128,256},{256,384},{1,129},{129,257},{257,385},{2,130},{1... | collective-permute-start | bytes 3080 | tf_op jit(solution)/shard_map/ppermute | solution.py:20
  348.0 6.9 %collective-permute-start.37 = (f32[16,16,1]{2,1,0:T(8,128)S(1)}, f32[16,16,1]{2,1,0:T(8,128)S(1)}, u32[]{:S(2)}, u32[]{:S(2)}) collective-permute-start(f32[16,16,1]{2,1,0:T(8,128)S(1)} %get-tuple-element.45), channel_id=1, source_target_pairs={{128,0},{256,128},{384,256},{129,1},{257,129},{385,257},{130,2},{2... | collective-permute-start | bytes 3080 | tf_op jit(solution)/shard_map/ppermute | solution.py:22
  355.0 4.3 %collective-permute-start.38 = (f32[1,16,130]{2,1,0:T(8,128)S(1)}, f32[1,16,130]{2,1,0:T(8,128)S(1)}, u32[]{:S(2)}, u32[]{:S(2)}) collective-permute-start(f32[1,16,130]{2,1,0:T(8,128)S(1)} %get-tuple-element.32), channel_id=1, source_target_pairs={{8,0},{16,8},{24,16},{32,24},{40,32},{48,40},{56,48},{64,56},{72,6... | collective-permute-start | bytes 24968 | tf_op jit(solution)/shard_map/ppermute | solution.py:22
  356.9 6.3 %collective-permute-start.39 = (f32[1,16,130]{2,1,0:T(8,128)S(1)}, f32[1,16,130]{2,1,0:T(8,128)S(1)}, u32[]{:S(2)}, u32[]{:S(2)}) collective-permute-start(f32[1,16,130]{2,1,0:T(8,128)S(1)} %get-tuple-element.31), channel_id=1, source_target_pairs={{0,8},{8,16},{16,24},{24,32},{32,40},{40,48},{48,56},{56,64},{64,7... | collective-permute-start | bytes 24968 | tf_op jit(solution)/shard_map/ppermute | solution.py:20
  363.3 6.1 %collective-permute-start.40 = (f32[18,1,130]{2,1,0:T(1,128)S(1)}, f32[18,1,130]{2,1,0:T(1,128)S(1)}, u32[]{:S(2)}, u32[]{:S(2)}) collective-permute-start(f32[18,1,130]{2,1,0:T(1,128)S(1)} %get-tuple-element.17), channel_id=1, source_target_pairs={{1,0},{2,1},{3,2},{4,3},{5,4},{6,5},{7,6},{9,8},{10,9},{11,10},{12... | collective-permute-start | bytes 28088 | tf_op jit(solution)/shard_map/ppermute | solution.py:22
  364.6 6.3 %collective-permute-start.41 = (f32[18,1,130]{2,1,0:T(1,128)S(1)}, f32[18,1,130]{2,1,0:T(1,128)S(1)}, u32[]{:S(2)}, u32[]{:S(2)}) collective-permute-start(f32[18,1,130]{2,1,0:T(1,128)S(1)} %get-tuple-element.18), channel_id=1, source_target_pairs={{0,1},{1,2},{2,3},{3,4},{4,5},{5,6},{6,7},{8,9},{9,10},{10,11},{11... | collective-permute-start | bytes 28088 | tf_op jit(solution)/shard_map/ppermute | solution.py:20
